TPU v7x, 512 devices: a whole 4x4x16 slice. The times are simulated.
512 devices in a mesh: pulse: 128 (over x, z, core), pol: 4 (over y).
Axes of the slice: x: 4, y: 4, z: 16, core: 2. Of those that a mesh axis runs over, the one named last changes fastest.
Arguments:
- echoes: bfloat16 [2, 4, 2048, 8192], P(None, 'pol', 'pulse'), may hold values from -6 to 6
- interp_weights: bfloat16 [64, 128, 128], replicated, may hold values from -0.5 to 0.5
- band_starts: int32 [64], replicated, may hold values from 0 to 8064, as said below
- row_lo: int32 [2048], P('pulse'), may hold values from 0 to 2047
- row_len: int32 [2048], P('pulse'), may hold values from 4098 to 8192, as said below
- tile_owner: int32 [4, 128, 512, 1], P('pol', 'pulse'), may hold values from 0 to 127; in each aligned block of 512 rows (0 to 511, 512 to 1023, ..., all dimensions but the last counted through in order) at most 8 rows name the same one
Outputs:
- coherency_tiles: float32 [10, 4, 128, 1024], P(None, 'pol', 'pulse')
Inputs may be any that keep to these rules, and one draw needn't show every extreme that they name: `band_starts`: Non-decreasing over the bands, the first 0 and the last 8064. row_lo + row_len never passes 8192. `tile_owner`: among the 512 tiles of one block (g, j), no owner is named more than 8 times.
All inputs are finite; a program needn't handle non-finite values.
Results may differ from a plain program's by a relative error of at most 0.0011.
Values may be sent and summed in bfloat16 or wider, within the bound.
A program may use at most 128 MiB of HBM per device.

v0:
```python
import math

import jax
import jax.numpy as jnp
import ml_dtypes
import numpy as np
from jax import lax
from jax.experimental import pallas as pl
from jax.experimental.pallas import tpu as pltpu
from jax.sharding import PartitionSpec as P

MESH = pl.DeviceIdType.MESH
ROOT_HALF = 1.0 / math.sqrt(2.0)
EPSILON = 1e-06
F32 = jnp.float32
BF16 = jnp.bfloat16

NX, NY, NZ, NC = 4, 4, 16, 2
PLANE = NX * NY * NC
GROUP = NX * NC
PULSES = 2048
ROWS = 1024
OWNERS = 128
TILES = 512
STEP = 16


def tables():
    row = np.arange(ROWS)
    azimuth = (row // 64 * 8 + row % 8) * 8 + row % 64 // 8
    z = np.arange(NZ)[:, None]
    k = np.arange(128)[None, :]
    pulse = (k // 32) * 512 + z * 32 + (k // 16 % 2) * 16 + k % 16
    m = azimuth[None, :, None] * pulse[:, None, :] % PULSES
    angles = m.astype(np.float32) * np.float32(2.0 * math.pi / PULSES)
    factor = np.float32(1.0 / math.sqrt(PULSES))
    both = np.concatenate([np.cos(angles) * factor, np.sin(angles) * factor], axis=2)
    return both.astype(ml_dtypes.bfloat16)


def selectors():
    sel = np.zeros((2, 16, 5, 2, 2, 4, 8), np.float32)
    for turn in range(2):
        for v in range(3):
            sel[turn, v, 0, :, turn, v] = 1
            sel[turn, 9, 0, :, turn, v] = 1
        for v, same, crossed, first in ((3, 1, 3, 0), (5, 2, 4, 0), (7, 1, 3, 1)):
            sel[turn, v, same, :, turn, first] = 1
            sel[turn, v + 1, crossed, 1, turn, first] = 1
            sel[turn, v + 1, crossed, 0, turn, first] = -1
    sel = sel.reshape(32, 640) / 64.0
    before = np.triu(np.ones((TILES, TILES), np.float32), 1)
    lanes = np.arange(128)
    spread = (np.arange(16)[:, None] == lanes[None, :] // 8) & (np.arange(16)[:, None] < 10)
    pick = np.concatenate([lanes[:, None] == v * 8 + lanes[None, :] % 8 for v in range(10)], axis=1)
    return [a.astype(ml_dtypes.bfloat16) for a in (sel, before, spread, pick)]


def split3(value):
    high = value.astype(BF16)
    rest = value - high.astype(F32)
    mid = rest.astype(BF16)
    low = (rest - mid.astype(F32)).astype(BF16)
    return high, mid, low


def swap_pieces(tiles, widths):
    lane = lax.broadcasted_iota(jnp.int32, (16, 128), 1) // 8
    tiles = list(tiles)
    for w in widths:
        upper = (lane & w) != 0
        for i in range(len(tiles)):
            if i & w:
                continue
            a, b = tiles[i], tiles[i | w]
            if a is None and b is None:
                continue
            a_down = 0.0 if a is None else pltpu.roll(a, 128 - 8 * w, 1)
            b_up = 0.0 if b is None else pltpu.roll(b, 8 * w, 1)
            tiles[i] = jnp.where(upper, b_up, 0.0 if a is None else a)
            tiles[i | w] = jnp.where(upper, 0.0 if b is None else b, a_down)
    return tiles


def resample_body(starts, lo, length, echo, weights, out):
    row = lax.broadcasted_iota(jnp.int32, (16, 128), 0)
    lane = lax.broadcasted_iota(jnp.int32, (16, 128), 1)
    lane2 = lax.broadcasted_iota(jnp.int32, (32, 128), 1)
    first = jnp.zeros((16, 128), jnp.int32)
    last = jnp.zeros((16, 128), jnp.int32)
    for r in range(16):
        first = jnp.where(row == r, lo[r], first)
        last = jnp.where(row == r, lo[r] + length[r], last)
    for n in range(STEP):
        band = pl.program_id(0) * STEP + n
        start = starts[band]
        base = jnp.minimum(start // 128, 62) * 128
        shift = start - base
        window = echo[:, :, pl.ds(pl.multiple_of(base, 128), 256)].astype(F32).reshape(32, 256)
        turn = (128 - shift) % 128
        left = pltpu.roll(window[:, :128], turn, 1)
        right = pltpu.roll(window[:, 128:], turn, 1)
        samples = jnp.where(lane2 < 128 - shift, left, right).astype(BF16)
        values = jnp.dot(samples, weights[n], preferred_element_type=F32).reshape(2, 16, 128)
        bins = band * 128 + lane
        inside = (bins >= first) & (bins < last)
        out[n] = jnp.where(inside[None], values, 0.0).astype(BF16)


def resample(echo, weights, starts, lo, length):
    smem = pl.BlockSpec(memory_space=pltpu.SMEM)
    return pl.pallas_call(
        resample_body,
        grid=(64 // STEP,),
        out_shape=jax.ShapeDtypeStruct((64, 2, 16, 128), BF16),
        in_specs=[
            smem,
            smem,
            smem,
            pl.BlockSpec((2, 16, 8192), lambda n: (0, 0, 0)),
            pl.BlockSpec((STEP, 128, 128), lambda n: (n, 0, 0)),
        ],
        out_specs=pl.BlockSpec((STEP, 2, 16, 128), lambda n: (n, 0, 0, 0)),
        compiler_params=pltpu.CompilerParams(vmem_limit_bytes=16 * 1024 * 1024),
    )(starts, lo, length, echo, weights)


def body(
    snd, owner, table, sel, before, spread, pick,
    out,
    tv, prcv, zsnd, zrcv, acc, sums, vout, grcv, onehot, slotmask, fsnd, frcv,
    load_sem, psend, precv, zsend, zrecv, gsend, grecv, fsend, frecv,
):
    pulse = lax.axis_index("pulse")
    y = lax.axis_index("pol")
    x, z, core = pulse // 32, pulse // 2 % 16, pulse % 2
    rank = x * 8 + y * 2 + core

    def plane_peer(k):
        px, py, pc = (x + k // 8) % 4, (y + k // 2 % 4) % 4, (core + k) % 2
        return ((px * 16 + z) * 2 + pc, py), px * 8 + py * 2 + pc

    def z_peer(k):
        pz = (z + k) % 16
        return ((x * 16 + pz) * 2 + core, y), pz

    load_t = pltpu.make_async_copy(table, tv, load_sem)
    load_t.start()

    barrier = pltpu.get_barrier_semaphore()

    @pl.loop(1, PLANE)
    def _(k):
        pl.semaphore_signal(barrier, inc=1, device_id=plane_peer(k)[0], device_id_type=MESH)

    @pl.loop(1, NZ)
    def _(k):
        pl.semaphore_signal(barrier, inc=1, device_id=z_peer(k)[0], device_id_type=MESH)

    row16 = lax.broadcasted_iota(jnp.int32, (16, 128), 0)
    lane16 = lax.broadcasted_iota(jnp.int32, (16, 128), 1)

    def plane_send(h):
        @pl.loop(1, PLANE)
        def _(k):
            device, to = plane_peer(k)
            pltpu.make_async_remote_copy(
                snd.at[2 * to + h], prcv.at[h, rank], psend.at[h], precv.at[h], device_id=device, device_id_type=MESH
            ).start()

        pltpu.make_async_copy(snd.at[2 * rank + h], prcv.at[h, rank], precv.at[h]).start()

    def plane_all(h, count):
        return pltpu.make_async_remote_copy(
            prcv.at[h, pl.ds(0, count)], prcv.at[h, pl.ds(0, count)], psend.at[h], precv.at[h],
            device_id=plane_peer(1)[0], device_id_type=MESH,
        )

    pl.semaphore_wait(barrier, PLANE - 1 + NZ - 1)
    plane_send(0)
    plane_send(1)

    def pack(h):
        plane_all(h, PLANE).wait_recv()
        for t in range(3):
            tiles = []
            for part in range(2):
                for g in range(GROUP):
                    def channel(q):
                        return prcv[h, g // 2 * 8 + q * 2 + g % 2, part].astype(F32)

                    if t == 0:
                        value = channel(0) + channel(3)
                    elif t == 1:
                        value = channel(0) - channel(3)
                    else:
                        value = channel(1) + channel(2)
                    tiles.append(value * ROOT_HALF)
            for to, tile in enumerate(swap_pieces(tiles, (1, 2, 4, 8))):
                zsnd[h, to, t] = tile.astype(BF16)

        @pl.loop(1, NZ)
        def _(k):
            device, to = z_peer(k)
            pltpu.make_async_remote_copy(
                zsnd.at[h, to], zrcv.at[h, z], zsend.at[h], zrecv.at[h, z], device_id=device, device_id_type=MESH
            ).start()

        zrcv[h, z] = zsnd[h, z]

    pack(0)
    pack(1)

    names = owner[...] == lax.broadcasted_iota(jnp.int32, (OWNERS, TILES), 0)
    mine = jnp.where(names, 1.0, 0.0).astype(BF16)
    onehot[...] = mine
    earlier = jnp.dot(mine, before[...], preferred_element_type=F32)
    earlier = jnp.where(names, earlier, 0.0).astype(BF16)
    slot = lax.dot_general(
        earlier, jnp.ones((OWNERS, 128), BF16), (((0,), (0,)), ((), ())), preferred_element_type=F32
    )
    lane_slot = (lax.broadcasted_iota(jnp.int32, (TILES, 128), 1) % 8).astype(F32)
    slotmask[...] = jnp.where(slot == lane_slot, 1.0, 0.0)
    load_t.wait()

    sign_row = (1 - 2 * (row16 % 2)).astype(F32)
    sign_part = jnp.where(lane16 < 64, 1.0, -1.0)

    def accumulate(h, source):
        tiles = [zrcv[h, source, t].astype(F32) for t in range(3)] + [None] * 5
        plain, turned = [], []
        for tile in swap_pieces(tiles, (1, 2, 4)):
            tile = tile + pltpu.roll(tile, 32, 1) * sign_row
            plain.append(tile.astype(BF16))
            turned.append((pltpu.roll(tile, 64, 1) * sign_part).astype(BF16))
        samples = jnp.concatenate(plain + turned, axis=0)
        return jnp.dot(tv[source], samples, preferred_element_type=F32)

    def form(h):
        acc[...] = accumulate(h, z)

        @pl.loop(1, NZ)
        def _(k):
            step = (k + 1) // 2
            source = (z + jnp.where(k % 2 == 1, step, 16 - step)) % 16
            pltpu.make_async_remote_copy(
                zsnd.at[h, 0], zrcv.at[h, source], zsend.at[h], zrecv.at[h, source],
                device_id=z_peer(1)[0], device_id_type=MESH,
            ).wait_recv()
            acc[...] += accumulate(h, source)

        @pl.loop(0, ROWS // 64)
        def _(k):
            a = acc[pl.ds(pl.multiple_of(k * 64, 64), 64), :]
            b1 = pltpu.roll(a, 120, 1)
            b2 = pltpu.roll(a, 112, 1)
            others = (a, b1, b2, pltpu.roll(b1, 64, 1), pltpu.roll(b2, 64, 1))
            for n, other in enumerate(others):
                sums[pl.ds(pl.multiple_of(k * 8, 8), 8), n * 128 : (n + 1) * 128] = jnp.sum(
                    (a * other).reshape(8, 8, 128), axis=0
                )

        entries = sum(
            lax.dot_general(sel[...], part, (((1,), (1,)), ((), ())), preferred_element_type=F32)
            for part in split3(sums[...])
        )
        for turn in range(2):
            entry = entries[turn * 16 : turn * 16 + 16]
            span = entry[9:10]
            scale = 1.0 / (span + EPSILON)
            vout[h, turn] = jnp.where(lax.broadcasted_iota(jnp.int32, (16, 128), 0) == 9, entry, entry * scale)

    def gather(h, action):
        for g in range(NY):
            device = (x * 32 + (y * 4 + core * 2 + h) * 2 + z // 8, jnp.int32(g))
            here = (device[0] == pulse) & (y == g)
            source, target = vout.at[h, 1 - g // 2], grcv.at[z % 8]

            @pl.when(jnp.logical_not(here))
            def _():
                copy = pltpu.make_async_remote_copy(
                    source, target, gsend, grecv, device_id=device, device_id_type=MESH
                )
                if action == "start":
                    copy.start()
                else:
                    copy.wait_send()

            if action == "start":

                @pl.when(here)
                def _():
                    pltpu.make_async_copy(source, target, grecv).start()

    for h in range(2):
        form(h)
        gather(h, "start")

    pltpu.make_async_remote_copy(grcv, grcv, gsend, grecv, device_id=plane_peer(1)[0], device_id_type=MESH).wait_recv()
    chunks = []
    odd = (y % 2) == 1
    for n in range(4):
        even_row, odd_row = grcv[2 * n], grcv[2 * n + 1]
        low = jnp.where(lane16 < 64, even_row, pltpu.roll(odd_row, 64, 1))
        high = jnp.where(lane16 < 64, pltpu.roll(even_row, 64, 1), odd_row)
        chunks.append(jnp.where(odd, high, low))
    values = jnp.concatenate(chunks, axis=1)
    wide = sum(
        lax.dot_general(part, spread[...], (((0,), (0,)), ((), ())), preferred_element_type=F32)
        for part in split3(values)
    )
    dealt = sum(
        jnp.dot(onehot[...], part, preferred_element_type=F32) for part in split3(wide * slotmask[...])
    )
    fsnd[...] = dealt.reshape(OWNERS, 1, 128)

    def place(p):
        return p % 16 * 8 + p // 16

    @pl.loop(1, OWNERS)
    def _(k):
        to = (pulse + k) % OWNERS
        pltpu.make_async_remote_copy(
            fsnd.at[to], frcv.at[place(pulse)], fsend, frecv, device_id=(to, y), device_id_type=MESH
        ).start()

    frcv[place(pulse)] = fsnd[pulse]
    final = pltpu.make_async_remote_copy(
        fsnd.at[pl.ds(0, OWNERS - 1)], frcv.at[pl.ds(0, OWNERS - 1)], fsend, frecv,
        device_id=plane_peer(1)[0], device_id_type=MESH,
    )
    final.wait_recv()
    arrived = frcv[...].reshape(OWNERS, 128)
    parts = split3(arrived)
    row = lax.broadcasted_iota(jnp.int32, (OWNERS, 128), 0)
    lane = lax.broadcasted_iota(jnp.int32, (OWNERS, 128), 1)
    own_lane = row // 8 == lane // 8
    for v in range(10):
        wide = sum(
            jnp.dot(part, pick[:, v * 128 : (v + 1) * 128], preferred_element_type=F32) for part in parts
        )
        out[v] = jnp.sum(jnp.where(own_lane, wide, 0.0).reshape(16, 8, 128), axis=0)

    for h in range(2):
        plane_all(h, PLANE - 1).wait_send()

        @pl.loop(1, NZ)
        def _(k):
            pltpu.make_async_remote_copy(
                zsnd.at[h, 0], zrcv.at[h, 0], zsend.at[h], zrecv.at[h, 0],
                device_id=z_peer(1)[0], device_id_type=MESH,
            ).wait_send()

        gather(h, "wait")
    final.wait_send()


def on_device(echoes, interp_weights, band_starts, row_lo, row_len, tile_owner):
    vmem = pl.BlockSpec(memory_space=pltpu.VMEM)
    hbm = pl.BlockSpec(memory_space=pl.ANY)
    sel, before, spread, pick = selectors()
    dma = pltpu.SemaphoreType.DMA
    annulus = resample(echoes.reshape(2, 16, 8192), interp_weights, band_starts, row_lo, row_len)
    moments = pl.pallas_call(
        body,
        out_shape=jax.ShapeDtypeStruct((10, 8, 128), F32),
        in_specs=[hbm, vmem, hbm, vmem, vmem, vmem, vmem],
        out_specs=vmem,
        scratch_shapes=[
            pltpu.VMEM((NZ, ROWS, 256), BF16),
            pltpu.VMEM((2, PLANE, 2, 16, 128), BF16),
            pltpu.VMEM((2, NZ, 3, 16, 128), BF16),
            pltpu.VMEM((2, NZ, 3, 16, 128), BF16),
            pltpu.VMEM((ROWS, 128), F32),
            pltpu.VMEM((128, 640), F32),
            pltpu.VMEM((2, 2, 16, 128), F32),
            pltpu.VMEM((8, 16, 128), F32),
            pltpu.VMEM((OWNERS, TILES), BF16),
            pltpu.VMEM((TILES, 128), F32),
            pltpu.VMEM((OWNERS, 1, 128), F32),
            pltpu.VMEM((OWNERS, 1, 128), F32),
            dma, dma((2,)), dma((2,)), dma((2,)), dma((2, NZ)), dma, dma, dma, dma,
        ],
        compiler_params=pltpu.CompilerParams(
            collective_id=0, has_side_effects=True, vmem_limit_bytes=48 * 1024 * 1024
        ),
    )(
        annulus,
        tile_owner.reshape(1, TILES),
        jnp.asarray(tables()),
        *[jnp.asarray(a) for a in (sel, before, spread, pick)],
    )
    return moments.reshape(10, 1, 1, 1024)


def solution(mesh):
    return jax.shard_map(
        on_device,
        mesh=mesh,
        in_specs=(
            P(None, "pol", "pulse", None),
            P(),
            P(),
            P("pulse"),
            P("pulse"),
            P("pol", "pulse", None, None),
        ),
        out_specs=P(None, "pol", "pulse", None),
        check_vma=False,
    )
```

profile of v0, /device:TPU:1, one launch (start us, length us, event | category | flops | bytes accessed | tf_op | source)
XLA Modules:
  0.0 94.0 jit_solution(2821373905044108900)
XLA Ops:
  0.0 0.0 copy-start
  0.0 1.6 %copy-done = bf16[64,128,128]{2,1,0:T(8,128)(2,1)S(1)} copy-done((bf16[64,128,128]{2,1,0:T(8,128)(2,1)S(1)}, bf16[64,128,128]{2,1,0:T(8,128)(2,1)}, u32[]{:S(2)}) %copy-start) | copy-done | bytes 2097176
  1.6 0.0 copy-start.1
  1.6 1.0 %copy-done.1 = bf16[2,1,16,8192]{3,2,1,0:T(8,128)(2,1)S(1)} copy-done((bf16[2,1,16,8192]{3,2,1,0:T(8,128)(2,1)S(1)}, bf16[2,1,16,8192]{3,2,1,0:T(8,128)(2,1)}, u32[]{:S(2)}) %copy-start.1) | copy-done | bytes 524312
  2.6 0.0 copy-start.7
  2.6 0.7 copy-done.7
  3.3 0.0 copy-start.8
  3.3 0.7 copy-done.8
  3.9 0.0 copy-start.9
  3.9 0.7 copy-done.9
  4.6 2.0 %shard_map.109.snd = bf16[64,2,16,128]{3,2,1,0:T(8,128)(2,1)S(1)} custom-call(s32[64]{0:T(128)S(1)} %copy-done.7, s32[16]{0:T(128)S(1)} %copy-done.8, s32[16]{0:T(128)S(1)} %copy-done.9, bf16[2,16,8192]{2,1,0:T(8,128)(2,1)S(1)} %bitcast.3, bf16[64,128,128]{2,1,0:T(8,128)(2,1)S(1)} %copy-done), custom_call_target="tpu_custom_call" | custom-call | tf_op jit(solution)/shard_map/pallas_call | solution.py:112
  6.6 0.0 copy-start.2
  6.6 1.0 %copy-done.2 = bf16[512,512]{1,0:T(8,128)(2,1)S(1)} copy-done((bf16[512,512]{1,0:T(8,128)(2,1)S(1)}, bf16[512,512]{1,0:T(8,128)(2,1)}, u32[]{:S(2)}) %copy-start.2) | copy-done | bytes 524312
  7.7 0.0 copy-start.3
  7.7 1.0 %copy-done.3 = bf16[128,1280]{1,0:T(8,128)(2,1)S(1)} copy-done((bf16[128,1280]{1,0:T(8,128)(2,1)S(1)}, bf16[128,1280]{1,0:T(8,128)(2,1)}, u32[]{:S(2)}) %copy-start.3) | copy-done | bytes 327704
  8.6 0.0 copy-start.4
  8.6 0.8 copy-done.4
  9.4 0.0 copy-start.5
  9.4 0.7 copy-done.5
  10.1 0.0 copy-start.6
  10.1 0.7 copy-done.6
  10.8 82.6 %shard_map.110 = f32[10,8,128]{2,1,0:T(8,128)S(1)} custom-call(bf16[64,2,16,128]{3,2,1,0:T(8,128)(2,1)S(1)} %shard_map.109.snd, s32[1,512]{1,0:T(1,128)S(1)} %bitcast.5, bf16[16,1024,256]{2,1,0:T(8,128)(2,1)} %constant.10.clone.table, bf16[32,640]{1,0:T(8,128)(2,1)S(1)} %copy-done.4, bf16[512,512]{1,0:T(8,128)(2,1)S(1)} %copy-done.2, ...), custom_call_target="tpu_custom_call" | custom-call | tf_op jit(solution)/shard_map/pallas_call | solution.py:364
  93.4 0.6 copy.15
Async XLA Ops:
  0.0 1.6 %copy-start = (bf16[64,128,128]{2,1,0:T(8,128)(2,1)S(1)}, bf16[64,128,128]{2,1,0:T(8,128)(2,1)}, u32[]{:S(2)}) copy-start(bf16[64,128,128]{2,1,0:T(8,128)(2,1)} %weights.1) | copy-start | bytes 6291460
  1.6 1.0 %copy-start.1 = (bf16[2,1,16,8192]{3,2,1,0:T(8,128)(2,1)S(1)}, bf16[2,1,16,8192]{3,2,1,0:T(8,128)(2,1)}, u32[]{:S(2)}) copy-start(bf16[2,1,16,8192]{3,2,1,0:T(8,128)(2,1)} %param.11) | copy-start | bytes 1572868
  2.6 0.7 copy-start.7
  3.3 0.7 copy-start.8
  3.9 0.7 copy-start.9
  6.6 1.0 %copy-start.2 = (bf16[512,512]{1,0:T(8,128)(2,1)S(1)}, bf16[512,512]{1,0:T(8,128)(2,1)}, u32[]{:S(2)}) copy-start(bf16[512,512]{1,0:T(8,128)(2,1)} %constant.12.clone.before) | copy-start | bytes 1572868
  7.7 1.0 %copy-start.3 = (bf16[128,1280]{1,0:T(8,128)(2,1)S(1)}, bf16[128,1280]{1,0:T(8,128)(2,1)}, u32[]{:S(2)}) copy-start(bf16[128,1280]{1,0:T(8,128)(2,1)} %constant.14.clone.pick) | copy-start | bytes 983044
  8.6 0.8 copy-start.4
  9.4 0.7 copy-start.5
  10.1 0.7 copy-start.6
where the time goes:
time: 94.4 us; the launch traced here: 94 us
  Pallas kernels  84.6 us (90%)
  local copies, waits for them, and re-layouts  9.37 us (10%)
    pallas_call x1, Pallas kernels, on_device(): pl.pallas_call(body, out_shape=jax.ShapeDtypeStruct((10, 8, 128), F32), i...  82.6 us
    unnamed x21, local copies, waits for them, and re-layouts  9.37 us
    pallas_call x1, Pallas kernels, resample(): pl.pallas_call(resample_body, grid=(64 // STEP,), out_shape=jax.ShapeDtyp...  2 us

commit v1 on v0

--- a/solution.py
+++ b/solution.py
@@ -23,6 +23,8 @@
 OWNERS = 128
 TILES = 512
 STEP = 16
+BATCH = 4
+VMEM_LIMIT = 60 * 1024 * 1024
 
 
 def tables():
@@ -39,19 +41,20 @@
 
 
 def selectors():
-    sel = np.zeros((2, 16, 5, 2, 2, 4, 8), np.float32)
+    sel = np.zeros((2, 2, 8, 5, 2, 2, 4, 8), np.float32)
     for turn in range(2):
         for v in range(3):
-            sel[turn, v, 0, :, turn, v] = 1
-            sel[turn, 9, 0, :, turn, v] = 1
+            sel[turn, v % 2, v // 2, 0, :, turn, v] = 1
+            sel[turn, 1, 4, 0, :, turn, v] = 1
         for v, same, crossed, first in ((3, 1, 3, 0), (5, 2, 4, 0), (7, 1, 3, 1)):
-            sel[turn, v, same, :, turn, first] = 1
-            sel[turn, v + 1, crossed, 1, turn, first] = 1
-            sel[turn, v + 1, crossed, 0, turn, first] = -1
+            sel[turn, 1, v // 2, same, :, turn, first] = 1
+            sel[turn, 0, (v + 1) // 2, crossed, 1, turn, first] = 1
+            sel[turn, 0, (v + 1) // 2, crossed, 0, turn, first] = -1
     sel = sel.reshape(32, 640) / 64.0
     before = np.triu(np.ones((TILES, TILES), np.float32), 1)
     lanes = np.arange(128)
-    spread = (np.arange(16)[:, None] == lanes[None, :] // 8) & (np.arange(16)[:, None] < 10)
+    rows = np.arange(16)[:, None]
+    spread = (rows % 8 * 2 + rows // 8 == lanes[None, :] // 8) & (rows % 8 < 5)
     pick = np.concatenate([lanes[:, None] == v * 8 + lanes[None, :] % 8 for v in range(10)], axis=1)
     return [a.astype(ml_dtypes.bfloat16) for a in (sel, before, spread, pick)]
 
@@ -75,60 +78,89 @@
             a, b = tiles[i], tiles[i | w]
             if a is None and b is None:
                 continue
-            a_down = 0.0 if a is None else pltpu.roll(a, 128 - 8 * w, 1)
-            b_up = 0.0 if b is None else pltpu.roll(b, 8 * w, 1)
-            tiles[i] = jnp.where(upper, b_up, 0.0 if a is None else a)
-            tiles[i | w] = jnp.where(upper, 0.0 if b is None else b, a_down)
+            zero = jnp.zeros_like(b if a is None else a)
+            a_down = zero if a is None else pltpu.roll(a, 128 - 8 * w, 1)
+            b_up = zero if b is None else pltpu.roll(b, 8 * w, 1)
+            tiles[i] = jnp.where(upper, b_up, zero if a is None else a)
+            tiles[i | w] = jnp.where(upper, zero if b is None else b, a_down)
     return tiles
 
 
-def resample_body(starts, lo, length, echo, weights, out):
+def resample_body(starts, lo, length, echo, weights, out, starts_s, lo_s, length_s, echo_v, weights_v, out_v, sem, wsem, osem):
+    smalls = [
+        pltpu.make_async_copy(source, target, sem.at[n])
+        for n, (source, target) in enumerate(((starts, starts_s), (lo, lo_s), (length, length_s), (echo, echo_v)))
+    ]
+    weight_copies = [
+        pltpu.make_async_copy(weights.at[pl.ds(n * STEP, STEP)], weights_v.at[pl.ds(n * STEP, STEP)], wsem.at[n])
+        for n in range(64 // STEP)
+    ]
+    for copy in smalls + weight_copies:
+        copy.start()
+    for copy in smalls:
+        copy.wait()
     row = lax.broadcasted_iota(jnp.int32, (16, 128), 0)
     lane = lax.broadcasted_iota(jnp.int32, (16, 128), 1)
     lane2 = lax.broadcasted_iota(jnp.int32, (32, 128), 1)
     first = jnp.zeros((16, 128), jnp.int32)
     last = jnp.zeros((16, 128), jnp.int32)
     for r in range(16):
-        first = jnp.where(row == r, lo[r], first)
-        last = jnp.where(row == r, lo[r] + length[r], last)
-    for n in range(STEP):
-        band = pl.program_id(0) * STEP + n
-        start = starts[band]
-        base = jnp.minimum(start // 128, 62) * 128
-        shift = start - base
-        window = echo[:, :, pl.ds(pl.multiple_of(base, 128), 256)].astype(F32).reshape(32, 256)
-        turn = (128 - shift) % 128
-        left = pltpu.roll(window[:, :128], turn, 1)
-        right = pltpu.roll(window[:, 128:], turn, 1)
-        samples = jnp.where(lane2 < 128 - shift, left, right).astype(BF16)
-        values = jnp.dot(samples, weights[n], preferred_element_type=F32).reshape(2, 16, 128)
-        bins = band * 128 + lane
-        inside = (bins >= first) & (bins < last)
-        out[n] = jnp.where(inside[None], values, 0.0).astype(BF16)
+        first = jnp.where(row == r, lo_s[r], first)
+        last = jnp.where(row == r, lo_s[r] + length_s[r], last)
+    out_copies = []
+    for step in range(64 // STEP):
+        weight_copies[step].wait()
+
+        @pl.loop(0, STEP, unroll=8)
+        def _(n):
+            band = step * STEP + n
+            start = starts_s[band]
+            base = jnp.minimum(start // 128, 62) * 128
+            shift = start - base
+            window = echo_v[:, :, pl.ds(pl.multiple_of(base, 128), 256)].astype(F32).reshape(32, 256)
+            turn = (128 - shift) % 128
+            left = pltpu.roll(window[:, :128], turn, 1)
+            right = pltpu.roll(window[:, 128:], turn, 1)
+            samples = jnp.where(lane2 < 128 - shift, left, right).astype(BF16)
+            values = jnp.dot(samples, weights_v[band], preferred_element_type=F32).reshape(2, 16, 128)
+            bins = band * 128 + lane
+            inside = (bins >= first) & (bins < last)
+            out_v[band] = jnp.where(inside[None], values, 0.0).astype(BF16)
+
+        copy = pltpu.make_async_copy(out_v.at[pl.ds(step * STEP, STEP)], out.at[pl.ds(step * STEP, STEP)], osem.at[step])
+        copy.start()
+        out_copies.append(copy)
+    for copy in out_copies:
+        copy.wait()
 
 
 def resample(echo, weights, starts, lo, length):
-    smem = pl.BlockSpec(memory_space=pltpu.SMEM)
+    hbm = pl.BlockSpec(memory_space=pl.ANY)
+    dma = pltpu.SemaphoreType.DMA
     return pl.pallas_call(
         resample_body,
-        grid=(64 // STEP,),
         out_shape=jax.ShapeDtypeStruct((64, 2, 16, 128), BF16),
-        in_specs=[
-            smem,
-            smem,
-            smem,
-            pl.BlockSpec((2, 16, 8192), lambda n: (0, 0, 0)),
-            pl.BlockSpec((STEP, 128, 128), lambda n: (n, 0, 0)),
+        in_specs=[hbm] * 5,
+        out_specs=hbm,
+        scratch_shapes=[
+            pltpu.SMEM((64,), jnp.int32),
+            pltpu.SMEM((16,), jnp.int32),
+            pltpu.SMEM((16,), jnp.int32),
+            pltpu.VMEM((2, 16, 8192), BF16),
+            pltpu.VMEM((64, 128, 128), BF16),
+            pltpu.VMEM((64, 2, 16, 128), BF16),
+            dma((4,)),
+            dma((64 // STEP,)),
+            dma((64 // STEP,)),
         ],
-        out_specs=pl.BlockSpec((STEP, 2, 16, 128), lambda n: (n, 0, 0, 0)),
-        compiler_params=pltpu.CompilerParams(vmem_limit_bytes=16 * 1024 * 1024),
+        compiler_params=pltpu.CompilerParams(vmem_limit_bytes=VMEM_LIMIT),
     )(starts, lo, length, echo, weights)
 
 
 def body(
-    snd, owner, table, sel, before, spread, pick,
+    snd, owner_h, table, sel_h, before_h, spread_h, pick_h,
     out,
-    tv, prcv, zsnd, zrcv, acc, sums, vout, grcv, onehot, slotmask, fsnd, frcv,
+    owner, tv, sel, before, spread, pick, prcv, zsnd, zrcv, acc, sums, vout, grcv, onehot, slotmask, fsnd, frcv,
     load_sem, psend, precv, zsend, zrecv, gsend, grecv, fsend, frecv,
 ):
     pulse = lax.axis_index("pulse")
@@ -137,15 +169,26 @@
     rank = x * 8 + y * 2 + core
 
     def plane_peer(k):
+        k = k * 5 % PLANE
         px, py, pc = (x + k // 8) % 4, (y + k // 2 % 4) % 4, (core + k) % 2
         return ((px * 16 + z) * 2 + pc, py), px * 8 + py * 2 + pc
 
+    def z_offset(k):
+        step = (17 - k) // 2
+        return jnp.where(k == 0, 0, jnp.where(k % 2 == 1, step, 16 - step))
+
     def z_peer(k):
-        pz = (z + k) % 16
+        pz = (z + z_offset(k)) % 16
         return ((x * 16 + pz) * 2 + core, y), pz
 
-    load_t = pltpu.make_async_copy(table, tv, load_sem)
-    load_t.start()
+    loads = [
+        pltpu.make_async_copy(source, target, load_sem.at[n])
+        for n, (source, target) in enumerate(
+            ((owner_h, owner), (before_h, before), (sel_h, sel), (spread_h, spread), (pick_h, pick), (table, tv))
+        )
+    ]
+    for load in loads:
+        load.start()
 
     barrier = pltpu.get_barrier_semaphore()
 
@@ -159,6 +202,8 @@
 
     row16 = lax.broadcasted_iota(jnp.int32, (16, 128), 0)
     lane16 = lax.broadcasted_iota(jnp.int32, (16, 128), 1)
+    row8 = lax.broadcasted_iota(jnp.int32, (8, 128), 0)
+    lane8 = lax.broadcasted_iota(jnp.int32, (8, 128), 1)
 
     def plane_send(h):
         @pl.loop(1, PLANE)
@@ -195,9 +240,9 @@
                         value = channel(0) - channel(3)
                     else:
                         value = channel(1) + channel(2)
-                    tiles.append(value * ROOT_HALF)
+                    tiles.append((value * ROOT_HALF).astype(BF16))
             for to, tile in enumerate(swap_pieces(tiles, (1, 2, 4, 8))):
-                zsnd[h, to, t] = tile.astype(BF16)
+                zsnd[h, to, t] = tile
 
         @pl.loop(1, NZ)
         def _(k):
@@ -206,11 +251,13 @@
                 zsnd.at[h, to], zrcv.at[h, z], zsend.at[h], zrecv.at[h, z], device_id=device, device_id_type=MESH
             ).start()
 
-        zrcv[h, z] = zsnd[h, z]
+        pltpu.make_async_copy(zsnd.at[h, z], zrcv.at[h, z], zrecv.at[h, z]).start()
 
     pack(0)
     pack(1)
 
+    for load in loads:
+        load.wait()
     names = owner[...] == lax.broadcasted_iota(jnp.int32, (OWNERS, TILES), 0)
     mine = jnp.where(names, 1.0, 0.0).astype(BF16)
     onehot[...] = mine
@@ -221,35 +268,40 @@
     )
     lane_slot = (lax.broadcasted_iota(jnp.int32, (TILES, 128), 1) % 8).astype(F32)
     slotmask[...] = jnp.where(slot == lane_slot, 1.0, 0.0)
-    load_t.wait()
-
-    sign_row = (1 - 2 * (row16 % 2)).astype(F32)
-    sign_part = jnp.where(lane16 < 64, 1.0, -1.0)
-
-    def accumulate(h, source):
-        tiles = [zrcv[h, source, t].astype(F32) for t in range(3)] + [None] * 5
+
+    sign_row = (1 - 2 * (row16 % 2)).astype(BF16)
+    sign_part = jnp.where(lane16 < 64, 1.0, -1.0).astype(BF16)
+
+    def samples_of(h, source):
+        tiles = [zrcv[h, source, t] for t in range(3)] + [None] * 5
         plain, turned = [], []
         for tile in swap_pieces(tiles, (1, 2, 4)):
             tile = tile + pltpu.roll(tile, 32, 1) * sign_row
-            plain.append(tile.astype(BF16))
-            turned.append((pltpu.roll(tile, 64, 1) * sign_part).astype(BF16))
-        samples = jnp.concatenate(plain + turned, axis=0)
-        return jnp.dot(tv[source], samples, preferred_element_type=F32)
+            plain.append(tile)
+            turned.append(pltpu.roll(tile, 64, 1) * sign_part)
+        return plain + turned
 
     def form(h):
-        acc[...] = accumulate(h, z)
-
-        @pl.loop(1, NZ)
-        def _(k):
-            step = (k + 1) // 2
-            source = (z + jnp.where(k % 2 == 1, step, 16 - step)) % 16
-            pltpu.make_async_remote_copy(
-                zsnd.at[h, 0], zrcv.at[h, source], zsend.at[h], zrecv.at[h, source],
-                device_id=z_peer(1)[0], device_id_type=MESH,
-            ).wait_recv()
-            acc[...] += accumulate(h, source)
-
-        @pl.loop(0, ROWS // 64)
+        acc[...] = jnp.zeros_like(acc)
+
+        @pl.loop(0, NZ // BATCH)
+        def _(group):
+            samples, waves = [], []
+            for n in range(BATCH):
+                source = (z + 16 - z_offset(group * BATCH + n)) % 16
+                pltpu.make_async_remote_copy(
+                    zsnd.at[h, 0], zrcv.at[h, source], zsend.at[h], zrecv.at[h, source],
+                    device_id=z_peer(1)[0], device_id_type=MESH,
+                ).wait_recv()
+            for n in range(BATCH):
+                source = (z + 16 - z_offset(group * BATCH + n)) % 16
+                samples += samples_of(h, source)
+                waves.append(tv[source])
+            acc[...] += jnp.dot(
+                jnp.concatenate(waves, axis=1), jnp.concatenate(samples, axis=0), preferred_element_type=F32
+            )
+
+        @pl.loop(0, ROWS // 64, unroll=4)
         def _(k):
             a = acc[pl.ds(pl.multiple_of(k * 64, 64), 64), :]
             b1 = pltpu.roll(a, 120, 1)
@@ -265,16 +317,18 @@
             for part in split3(sums[...])
         )
         for turn in range(2):
-            entry = entries[turn * 16 : turn * 16 + 16]
-            span = entry[9:10]
-            scale = 1.0 / (span + EPSILON)
-            vout[h, turn] = jnp.where(lax.broadcasted_iota(jnp.int32, (16, 128), 0) == 9, entry, entry * scale)
+            even, odd = entries[turn * 16 : turn * 16 + 8], entries[turn * 16 + 8 : turn * 16 + 16]
+            scale = 1.0 / (odd[4:5] + EPSILON)
+            even = even * scale
+            odd = jnp.where(row8 == 4, odd, odd * scale)
+            vout[h, 2 - 2 * turn] = jnp.where(lane8 < 64, even, pltpu.roll(odd, 64, 1))
+            vout[h, 3 - 2 * turn] = jnp.where(lane8 < 64, pltpu.roll(even, 64, 1), odd)
 
     def gather(h, action):
         for g in range(NY):
             device = (x * 32 + (y * 4 + core * 2 + h) * 2 + z // 8, jnp.int32(g))
             here = (device[0] == pulse) & (y == g)
-            source, target = vout.at[h, 1 - g // 2], grcv.at[z % 8]
+            source, target = vout.at[h, g], grcv.at[z % 8]
 
             @pl.when(jnp.logical_not(here))
             def _():
@@ -297,14 +351,12 @@
         gather(h, "start")
 
     pltpu.make_async_remote_copy(grcv, grcv, gsend, grecv, device_id=plane_peer(1)[0], device_id_type=MESH).wait_recv()
-    chunks = []
-    odd = (y % 2) == 1
+    evens, odds = [], []
     for n in range(4):
-        even_row, odd_row = grcv[2 * n], grcv[2 * n + 1]
-        low = jnp.where(lane16 < 64, even_row, pltpu.roll(odd_row, 64, 1))
-        high = jnp.where(lane16 < 64, pltpu.roll(even_row, 64, 1), odd_row)
-        chunks.append(jnp.where(odd, high, low))
-    values = jnp.concatenate(chunks, axis=1)
+        one, two = grcv[2 * n], grcv[2 * n + 1]
+        evens.append(jnp.where(lane8 < 64, one, pltpu.roll(two, 64, 1)))
+        odds.append(jnp.where(lane8 < 64, pltpu.roll(one, 64, 1), two))
+    values = jnp.concatenate([jnp.concatenate(evens, axis=1), jnp.concatenate(odds, axis=1)], axis=0)
     wide = sum(
         lax.dot_general(part, spread[...], (((0,), (0,)), ((), ())), preferred_element_type=F32)
         for part in split3(values)
@@ -364,25 +416,30 @@
     moments = pl.pallas_call(
         body,
         out_shape=jax.ShapeDtypeStruct((10, 8, 128), F32),
-        in_specs=[hbm, vmem, hbm, vmem, vmem, vmem, vmem],
+        in_specs=[hbm] * 7,
         out_specs=vmem,
         scratch_shapes=[
+            pltpu.VMEM((1, TILES), jnp.int32),
             pltpu.VMEM((NZ, ROWS, 256), BF16),
+            pltpu.VMEM((32, 640), BF16),
+            pltpu.VMEM((TILES, TILES), BF16),
+            pltpu.VMEM((16, 128), BF16),
+            pltpu.VMEM((128, 1280), BF16),
             pltpu.VMEM((2, PLANE, 2, 16, 128), BF16),
             pltpu.VMEM((2, NZ, 3, 16, 128), BF16),
             pltpu.VMEM((2, NZ, 3, 16, 128), BF16),
             pltpu.VMEM((ROWS, 128), F32),
             pltpu.VMEM((128, 640), F32),
-            pltpu.VMEM((2, 2, 16, 128), F32),
-            pltpu.VMEM((8, 16, 128), F32),
+            pltpu.VMEM((2, NY, 8, 128), F32),
+            pltpu.VMEM((8, 8, 128), F32),
             pltpu.VMEM((OWNERS, TILES), BF16),
             pltpu.VMEM((TILES, 128), F32),
             pltpu.VMEM((OWNERS, 1, 128), F32),
             pltpu.VMEM((OWNERS, 1, 128), F32),
-            dma, dma((2,)), dma((2,)), dma((2,)), dma((2, NZ)), dma, dma, dma, dma,
+            dma((6,)), dma((2,)), dma((2,)), dma((2,)), dma((2, NZ)), dma, dma, dma, dma,
         ],
         compiler_params=pltpu.CompilerParams(
-            collective_id=0, has_side_effects=True, vmem_limit_bytes=48 * 1024 * 1024
+            collective_id=0, has_side_effects=True, vmem_limit_bytes=VMEM_LIMIT
         ),
     )(
         annulus,

time: 94.4 us -> 74.5 us (0.79)
  Pallas kernels: 84.6 us -> 72.9 us
  local copies, waits for them, and re-layouts: 9.37 us -> 1.4 us
    pallas_call x1, Pallas kernels: 82.6 us -> 68.5 us  [on_device(): pl.pallas_call(body, out_shape=jax.ShapeDtypeStruct((10, 8, 128), F32), i...]
    unnamed x21 -> x1, local copies, waits for them, and re-layouts: 9.37 us -> 1.4 us
    pallas_call x1, Pallas kernels: 2 us -> 4.38 us  [resample(): pl.pallas_call(resample_body, out_shape=jax.ShapeDtypeStruct((64, 2, 16,...]
where the time goes in v1:
time: 74.5 us; the launch traced here: 74.3 us
  Pallas kernels  72.9 us (98%)
  local copies, waits for them, and re-layouts  1.4 us (2%)
    pallas_call x1, Pallas kernels, on_device(): pl.pallas_call(body, out_shape=jax.ShapeDtypeStruct((10, 8, 128), F32), i...  68.5 us
    pallas_call x1, Pallas kernels, resample(): pl.pallas_call(resample_body, out_shape=jax.ShapeDtypeStruct((64, 2, 16,...  4.38 us

profile of v1, /device:TPU:1, one launch (start us, length us, event | category | flops | bytes accessed | tf_op | source)
XLA Modules:
  0.0 74.3 jit_solution(3997236872756611867)
XLA Ops:
  0.0 4.4 %shard_map.109.snd = bf16[64,2,16,128]{3,2,1,0:T(8,128)(2,1)} custom-call(s32[64]{0:T(128)} %starts.1, s32[16]{0:T(128)} %lo.1, s32[16]{0:T(128)} %length.1, bf16[2,16,8192]{2,1,0:T(8,128)(2,1)} %bitcast.3, bf16[64,128,128]{2,1,0:T(8,128)(2,1)} %weights.1), custom_call_target="tpu_custom_call" | custom-call | tf_op jit(solution)/shard_map/pallas_call | solution.py:140
  4.4 68.5 %shard_map.110 = f32[10,8,128]{2,1,0:T(8,128)} custom-call(bf16[64,2,16,128]{3,2,1,0:T(8,128)(2,1)} %shard_map.109.snd, s32[1,512]{1,0:T(1,128)} %bitcast.5, bf16[16,1024,256]{2,1,0:T(8,128)(2,1)} %constant.10.clone.table, bf16[32,640]{1,0:T(8,128)(2,1)} %constant.11.clone.sel_h, bf16[512,512]{1,0:T(8,128)(2,1)} %constant.12.clone.before_h, ...), custom_call_target="tpu_custom_call" | custom-call | tf_op jit(solution)/shard_map/pallas_call | solution.py:416
  72.9 1.4 %copy.15 = f32[10,1,1,1024]{3,2,1,0:T(1,128)} copy(f32[10,1,1,1024]{3,2,1,0:T(1,128)} %bitcast.4) | data formatting | bytes 81920

commit v2 on v1

--- a/solution.py
+++ b/solution.py
@@ -57,6 +57,14 @@
     spread = (rows % 8 * 2 + rows // 8 == lanes[None, :] // 8) & (rows % 8 < 5)
     pick = np.concatenate([lanes[:, None] == v * 8 + lanes[None, :] % 8 for v in range(10)], axis=1)
     return [a.astype(ml_dtypes.bfloat16) for a in (sel, before, spread, pick)]
+
+
+def rem(a, b):
+    return lax.rem(a, jnp.int32(b))
+
+
+def div(a, b):
+    return lax.div(a, jnp.int32(b))
 
 
 def split3(value):
@@ -111,7 +119,7 @@
     for step in range(64 // STEP):
         weight_copies[step].wait()
 
-        @pl.loop(0, STEP, unroll=8)
+        @pl.loop(0, STEP, unroll=16)
         def _(n):
             band = step * STEP + n
             start = starts_s[band]
@@ -169,16 +177,17 @@
     rank = x * 8 + y * 2 + core
 
     def plane_peer(k):
-        k = k * 5 % PLANE
-        px, py, pc = (x + k // 8) % 4, (y + k // 2 % 4) % 4, (core + k) % 2
+        k = rem(jnp.int32(k) * 5, PLANE)
+        px, py, pc = rem(x + div(k, 8), 4), rem(y + div(k, 2), 4), rem(core + k, 2)
         return ((px * 16 + z) * 2 + pc, py), px * 8 + py * 2 + pc
 
     def z_offset(k):
-        step = (17 - k) // 2
-        return jnp.where(k == 0, 0, jnp.where(k % 2 == 1, step, 16 - step))
+        k = jnp.int32(k)
+        step = div(17 - k, 2)
+        return jnp.where(k == 0, 0, jnp.where(rem(k, 2) == 1, step, 16 - step))
 
     def z_peer(k):
-        pz = (z + z_offset(k)) % 16
+        pz = rem(z + z_offset(k), 16)
         return ((x * 16 + pz) * 2 + core, y), pz
 
     loads = [
@@ -288,13 +297,13 @@
         def _(group):
             samples, waves = [], []
             for n in range(BATCH):
-                source = (z + 16 - z_offset(group * BATCH + n)) % 16
+                source = rem(z + 16 - z_offset(group * BATCH + n), 16)
                 pltpu.make_async_remote_copy(
                     zsnd.at[h, 0], zrcv.at[h, source], zsend.at[h], zrecv.at[h, source],
                     device_id=z_peer(1)[0], device_id_type=MESH,
                 ).wait_recv()
             for n in range(BATCH):
-                source = (z + 16 - z_offset(group * BATCH + n)) % 16
+                source = rem(z + 16 - z_offset(group * BATCH + n), 16)
                 samples += samples_of(h, source)
                 waves.append(tv[source])
             acc[...] += jnp.dot(
@@ -369,14 +378,16 @@
     def place(p):
         return p % 16 * 8 + p // 16
 
+    here = place(pulse)
+
     @pl.loop(1, OWNERS)
     def _(k):
-        to = (pulse + k) % OWNERS
+        to = rem(pulse + k, OWNERS)
         pltpu.make_async_remote_copy(
-            fsnd.at[to], frcv.at[place(pulse)], fsend, frecv, device_id=(to, y), device_id_type=MESH
+            fsnd.at[to], frcv.at[here], fsend, frecv, device_id=(to, y), device_id_type=MESH
         ).start()
 
-    frcv[place(pulse)] = fsnd[pulse]
+    frcv[here] = fsnd[pulse]
     final = pltpu.make_async_remote_copy(
         fsnd.at[pl.ds(0, OWNERS - 1)], frcv.at[pl.ds(0, OWNERS - 1)], fsend, frecv,
         device_id=plane_peer(1)[0], device_id_type=MESH,

time: 74.5 us -> 73.3 us (0.984)
  Pallas kernels: 72.9 us -> 71.7 us
where the time goes in v2:
time: 73.3 us; the launch traced here: 73.1 us
  Pallas kernels  71.7 us (98%)
  local copies, waits for them, and re-layouts  1.4 us (2%)
    pallas_call x1, Pallas kernels, on_device(): pl.pallas_call(body, out_shape=jax.ShapeDtypeStruct((10, 8, 128), F32), i...  68 us
    pallas_call x1, Pallas kernels, resample(): pl.pallas_call(resample_body, out_shape=jax.ShapeDtypeStruct((64, 2, 16,...  3.69 us

profile of v2, /device:TPU:1, one launch (start us, length us, event | category | flops | bytes accessed | tf_op | source)
XLA Modules:
  0.0 73.1 jit_solution(3398184045658123072)
XLA Ops:
  0.0 3.7 %shard_map.109.snd = bf16[64,2,16,128]{3,2,1,0:T(8,128)(2,1)} custom-call(s32[64]{0:T(128)} %starts.1, s32[16]{0:T(128)} %lo.1, s32[16]{0:T(128)} %length.1, bf16[2,16,8192]{2,1,0:T(8,128)(2,1)} %bitcast.3, bf16[64,128,128]{2,1,0:T(8,128)(2,1)} %weights.1), custom_call_target="tpu_custom_call" | custom-call | tf_op jit(solution)/shard_map/pallas_call | solution.py:148
  3.7 68.0 %shard_map.110 = f32[10,8,128]{2,1,0:T(8,128)} custom-call(bf16[64,2,16,128]{3,2,1,0:T(8,128)(2,1)} %shard_map.109.snd, s32[1,512]{1,0:T(1,128)} %bitcast.5, bf16[16,1024,256]{2,1,0:T(8,128)(2,1)} %constant.10.clone.table, bf16[32,640]{1,0:T(8,128)(2,1)} %constant.11.clone.sel_h, bf16[512,512]{1,0:T(8,128)(2,1)} %constant.12.clone.before_h, ...), custom_call_target="tpu_custom_call" | custom-call | tf_op jit(solution)/shard_map/pallas_call | solution.py:427
  71.7 1.4 %copy.15 = f32[10,1,1,1024]{3,2,1,0:T(1,128)} copy(f32[10,1,1,1024]{3,2,1,0:T(1,128)} %bitcast.4) | data formatting | bytes 81920

commit v3 on v2

--- a/solution.py
+++ b/solution.py
@@ -392,6 +392,17 @@
         fsnd.at[pl.ds(0, OWNERS - 1)], frcv.at[pl.ds(0, OWNERS - 1)], fsend, frecv,
         device_id=plane_peer(1)[0], device_id_type=MESH,
     )
+    for h in range(2):
+        plane_all(h, PLANE - 1).wait_send()
+
+        @pl.loop(1, NZ)
+        def _(k):
+            pltpu.make_async_remote_copy(
+                zsnd.at[h, 0], zrcv.at[h, 0], zsend.at[h], zrecv.at[h, 0],
+                device_id=z_peer(1)[0], device_id_type=MESH,
+            ).wait_send()
+
+        gather(h, "wait")
     final.wait_recv()
     arrived = frcv[...].reshape(OWNERS, 128)
     parts = split3(arrived)
@@ -404,17 +415,6 @@
         )
         out[v] = jnp.sum(jnp.where(own_lane, wide, 0.0).reshape(16, 8, 128), axis=0)
 
-    for h in range(2):
-        plane_all(h, PLANE - 1).wait_send()
-
-        @pl.loop(1, NZ)
-        def _(k):
-            pltpu.make_async_remote_copy(
-                zsnd.at[h, 0], zrcv.at[h, 0], zsend.at[h], zrecv.at[h, 0],
-                device_id=z_peer(1)[0], device_id_type=MESH,
-            ).wait_send()
-
-        gather(h, "wait")
     final.wait_send()
 
 

time: 73.3 us -> 73.2 us (level)
  no operation moved by 1% of the time
where the time goes in v3:
time: 73.2 us; the launch traced here: 73 us
  Pallas kernels  71.5 us (98%)
  local copies, waits for them, and re-layouts  1.4 us (2%)
    pallas_call x1, Pallas kernels, on_device(): pl.pallas_call(body, out_shape=jax.ShapeDtypeStruct((10, 8, 128), F32), i...  67.8 us
    pallas_call x1, Pallas kernels, resample(): pl.pallas_call(resample_body, out_shape=jax.ShapeDtypeStruct((64, 2, 16,...  3.69 us

profile of v3, /device:TPU:1, one launch (start us, length us, event | category | flops | bytes accessed | tf_op | source)
XLA Modules:
  0.0 73.0 jit_solution(18226889697956245930)
XLA Ops:
  0.0 3.7 %shard_map.109.snd = bf16[64,2,16,128]{3,2,1,0:T(8,128)(2,1)} custom-call(s32[64]{0:T(128)} %starts.1, s32[16]{0:T(128)} %lo.1, s32[16]{0:T(128)} %length.1, bf16[2,16,8192]{2,1,0:T(8,128)(2,1)} %bitcast.3, bf16[64,128,128]{2,1,0:T(8,128)(2,1)} %weights.1), custom_call_target="tpu_custom_call" | custom-call | tf_op jit(solution)/shard_map/pallas_call | solution.py:148
  3.7 67.8 %shard_map.110 = f32[10,8,128]{2,1,0:T(8,128)} custom-call(bf16[64,2,16,128]{3,2,1,0:T(8,128)(2,1)} %shard_map.109.snd, s32[1,512]{1,0:T(1,128)} %bitcast.5, bf16[16,1024,256]{2,1,0:T(8,128)(2,1)} %constant.10.clone.table, bf16[32,640]{1,0:T(8,128)(2,1)} %constant.11.clone.sel_h, bf16[512,512]{1,0:T(8,128)(2,1)} %constant.12.clone.before_h, ...), custom_call_target="tpu_custom_call" | custom-call | tf_op jit(solution)/shard_map/pallas_call | solution.py:427
  71.6 1.4 %copy.15 = f32[10,1,1,1024]{3,2,1,0:T(1,128)} copy(f32[10,1,1,1024]{3,2,1,0:T(1,128)} %bitcast.4) | data formatting | bytes 81920
